TPU v7x, 512 devices: a whole 4x8x8 slice. The times are simulated.
512 devices in a mesh: row: 16 (over y, core), col: 32 (over x, z).
Axes of the slice: x: 4, y: 8, z: 8, core: 2. Of those that a mesh axis runs over, the one named last changes fastest.
Arguments:
- pointing_dirty_images: bfloat16 [512, 1024, 1024], P(('row', 'col')), may hold values from -6 to 6
- beam_coefs: bfloat16 [512, 36], P(('row', 'col'))
- pointing_offsets: int32 [512, 2], P(('row', 'col')), may hold values from 0 to 60, as said below
Outputs:
- joint_image: bfloat16 [64, 32, 256, 256], P('row', 'col')
- residual: bfloat16 [512, 1024, 1024], P(('row', 'col'))
Inputs may be any that keep to these rules, and one draw needn't show every extreme that they name: `pointing_offsets`: for a pointing p in group g = p // 32: the tile row lies in 4 g .. 4 g + 3, and equals 4 g in the last group; the tile column lies in 0 .. 28; the first pointing of each group has column 0 and the second column 28.
All inputs are finite; a program needn't handle non-finite values.
Results may differ from a plain program's by a relative error of at most 0.005.
Values may be sent and summed in bfloat16 or wider, within the bound.
A program may use at most 128 MiB of HBM per device.

v0:
```python
import math

import jax
import jax.numpy as jnp
import numpy as np
from jax import lax
from jax.sharding import PartitionSpec as P

FT = 4


weight_floor = 0.1


def shifted(value, axis, by):
    devices = lax.axis_size(axis)
    pairs = [(i, i + by) for i in range(devices) if 0 <= i + by < devices]
    return lax.ppermute(value, axis, pairs)


def zernike_table():
    table = np.zeros((36, 8, 8))
    term = 0
    for degree in range(8):
        for azimuth in range(-degree, degree + 1, 2):
            order = abs(azimuth)
            angular = np.zeros((8, 8))
            for power in range(order + 1):
                weight = math.comb(order, power)
                if azimuth >= 0 and power % 2 == 0:
                    angular[order - power, power] += weight * (-1) ** (power // 2)
                if azimuth < 0 and power % 2 == 1:
                    angular[order - power, power] += weight * (-1) ** ((power - 1) // 2)
            for stepper in range((degree - order) // 2 + 1):
                radial = (
                    (-1) ** stepper
                    * math.factorial(degree - stepper)
                    / (
                        math.factorial(stepper)
                        * math.factorial((degree + order) // 2 - stepper)
                        * math.factorial((degree - order) // 2 - stepper)
                    )
                )
                square_power = (degree - 2 * stepper - order) // 2
                for portion in range(square_power + 1):
                    factor = radial * math.comb(square_power, portion)
                    shift_u = 2 * portion
                    shift_v = 2 * (square_power - portion)
                    table[term, shift_u:, shift_v:] += (
                        factor * angular[: 8 - shift_u, : 8 - shift_v]
                    )
            term += 1
    return table


def positions(start, count, footprint):
    pixels = start + jnp.arange(count, dtype=jnp.float32)
    return (pixels + 0.5 - footprint / 2.0) * (math.sqrt(2.0) / footprint)


def beam_power(coef, table, across, shift_downward_step):
    monomial_term = jnp.einsum(
        "k,kab->ab", coef.astype(jnp.float32), table, precision=lax.Precision.HIGHEST
    )
    exponent_value = jnp.arange(8, dtype=jnp.float32)
    upow = across[None, :] ** exponent_value[:, None]
    vertical_power = shift_downward_step[None, :] ** exponent_value[:, None]
    left_neighbour = jnp.dot(vertical_power.T, monomial_term.T, precision=lax.Precision.HIGHEST)
    field = jnp.dot(left_neighbour, upow, precision=lax.Precision.HIGHEST)
    return (field * field).astype(jnp.bfloat16)


def split_tiles(picture):
    side = picture.shape[0] // FT
    return picture.reshape(FT, side, FT, side).transpose(0, 2, 1, 3).reshape(FT * FT, side, side)


def join_tiles(tiles):
    side = tiles.shape[1]
    return tiles.reshape(FT, FT, side, side).transpose(0, 2, 1, 3).reshape(FT * side, FT * side)


def local(pointing_dirty_images, beam_coefs, pointing_offsets):
    col_count = lax.axis_size("col")
    capacity = max(1, 16 // col_count)
    slot_total = col_count * capacity
    group = lax.axis_index("row")
    footprint = pointing_dirty_images.shape[1]
    tile_size = footprint // FT
    table = jnp.asarray(zernike_table(), jnp.float32)
    picture = pointing_dirty_images[0]
    coef = beam_coefs[0]
    top_row = pointing_offsets[0, 0]
    left_col = pointing_offsets[0, 1]
    counter = jnp.arange(FT * FT, dtype=jnp.int32)
    tile_row = counter // FT
    tile_column_index = counter % FT
    rows_abs = top_row + tile_row
    dest_col = (left_col + tile_column_index + FT * rows_abs) % col_count
    slot_index = counter // col_count
    flat_index = dest_col * capacity + slot_index
    targets = (rows_abs - FT * group).astype(jnp.float32)
    empty_target = float(2 * FT - 1)
    values = split_tiles(picture)
    blank = jnp.zeros((slot_total, tile_size, tile_size), jnp.bfloat16)
    send_values = (
        blank.at[flat_index].set(values).reshape(col_count, capacity, tile_size, tile_size)
    )
    across = positions(0.0, footprint, footprint)
    power = split_tiles(beam_power(coef, table, across, across))
    send_power = blank.at[flat_index].set(power).reshape(col_count, capacity, tile_size, tile_size)
    send_meta = jnp.full((slot_total,), empty_target, jnp.float32).at[flat_index].set(targets)
    send_meta = send_meta.astype(jnp.bfloat16).reshape(col_count, capacity)
    got_values, got_power, got_meta = (
        lax.all_to_all(send_values, "col", split_axis=0, concat_axis=0, tiled=True),
        lax.all_to_all(send_power, "col", split_axis=0, concat_axis=0, tiled=True),
        lax.all_to_all(send_meta, "col", split_axis=0, concat_axis=0, tiled=True),
    )
    got_target = got_meta.reshape(slot_total).astype(jnp.float32)
    got_power = got_power.reshape(slot_total, tile_size, tile_size)
    got_values = got_values.reshape(slot_total, tile_size, tile_size).astype(jnp.float32)
    power_wide = got_power.astype(jnp.float32)
    onehot = (got_target[:, None] == jnp.arange(2 * FT - 1, dtype=jnp.float32)[None, :]).astype(
        jnp.float32
    )
    numer = jnp.einsum(
        "st,sxy->txy", onehot, got_values * power_wide, precision=lax.Precision.HIGHEST
    )
    weigh = jnp.einsum(
        "st,sxy->txy", onehot, power_wide * power_wide, precision=lax.Precision.HIGHEST
    )
    lower = jnp.stack([numer[FT:], weigh[FT:]])
    moved = shifted(lower, "row", 1)
    filler = jnp.zeros((1, tile_size, tile_size), jnp.float32)
    numer_own = numer[:FT] + jnp.concatenate([moved[0], filler])
    weight_own_pointing = weigh[:FT] + jnp.concatenate([moved[1], filler])
    joint_image = (numer_own / jnp.maximum(weight_own_pointing, weight_floor)).astype(jnp.bfloat16)
    above = shifted(joint_image[: FT - 1], "row", -1)
    extended = jnp.concatenate([joint_image, above])
    backward = jnp.einsum(
        "st,txy->sxy", onehot.astype(jnp.bfloat16), extended, preferred_element_type=jnp.float32
    ).astype(jnp.bfloat16)
    returned = lax.all_to_all(
        backward.reshape(col_count, capacity, tile_size, tile_size),
        "col",
        split_axis=0,
        concat_axis=0,
        tiled=True,
    )
    model = returned.reshape(slot_total, tile_size, tile_size)[flat_index].astype(jnp.float32)
    remainder = (values.astype(jnp.float32) - power.astype(jnp.float32) * model).astype(
        jnp.bfloat16
    )
    return (joint_image.reshape(FT, 1, tile_size, tile_size), join_tiles(remainder)[None])


def solution(mesh):
    in_specs = (P(("row", "col"), None, None), P(("row", "col"), None), P(("row", "col"), None))
    out_specs = (P("row", "col", None, None), P(("row", "col"), None, None))
    return jax.shard_map(local, mesh=mesh, in_specs=in_specs, out_specs=out_specs, check_vma=False)
```

profile of v0, /device:TPU:47, one launch (start us, length us, event | category | flops | bytes accessed | tf_op | source)
XLA Modules:
  0.0 436.6 jit_solution(14924420058807439925)
XLA Ops:
  0.6 0.0 copy-start
  0.7 1.3 fusion.42
  2.0 1.3 fusion.35
  3.3 0.7 fusion.29
  3.9 0.6 scatter_custom_fusion
  4.6 0.7 copy.30
  5.3 12.9 %all-to-all-start = ((bf16[32,1,1]{2,1,0:T(2,128)(2,1)}), bf16[32,1,1]{2,1,0:T(2,128)(2,1)S(1)}, u32[]{:S(2)}, u32[]{:S(2)}) async-start(bf16[32,1,1]{2,1,0:T(2,128)(2,1)} %copy.30), calls=%async_computation | async-start | bytes 32768 | tf_op jit(solution)/shard_map/all_to_all | solution.py:117
  18.2 1.1 fusion.36
  19.3 0.2 fusion.15
  19.5 4.7 %multiply_convert_fusion = bf16[1024,1024]{1,0:T(8,128)(2,1)} fusion(f32[1024,8]{0,1:T(8,128)S(1)} %fusion.15, f32[1024]{0:T(1024)S(1)} %add_multiply_fusion), kind=kOutput, calls=%fused_computation.16 | convolution fusion | flops 102760448 | bytes 2134016 | tf_op jit(solution)/shard_map/dot_general | solution.py:69
  24.2 3.3 reshape.186
  27.6 1.7 copy.33
  29.2 2.4 broadcast_in_dim.5.clone
  31.7 6.0 %scatter_fusion.1 = bf16[32,256,256]{2,1,0:T(8,128)(2,1)} fusion(bf16[32,256,256]{2,1,0:T(8,128)(2,1)} %broadcast_in_dim.5.clone, s32[16]{0:T(128)S(1)} %fusion.35, bf16[16,256,256]{2,1,0:T(8,128)(2,1)} %bitcast.64), kind=kCustom, calls=%fused_computation.3 | custom fusion | bytes 6291520 | tf_op jit(solution)/shard_map/scatter | solution.py:111
  37.7 0.0 all-to-all-done
  37.7 9.3 %all-to-all-start.2 = ((bf16[32,1,256,256]{3,2,1,0:T(8,128)(2,1)}), bf16[32,1,256,256]{3,2,1,0:T(8,128)(2,1)}, u32[]{:S(2)}, u32[]{:S(2)}) async-start(bf16[32,1,256,256]{3,2,1,0:T(8,128)(2,1)} %bitcast.59), calls=%async_computation.2 | async-start | bytes 8388608 | tf_op jit(solution)/shard_map/all_to_all | solution.py:116
  46.9 4.5 %reshape_squeeze.3 = bf16[4,256,4,256]{3,2,1,0:T(4,128)(2,1)} reshape(bf16[1,1024,1024]{2,1,0:T(8,128)(2,1)} %param.4) | data formatting | bytes 4194304 | tf_op jit(solution)/shard_map/reshape;squeeze | solution.py:75
  51.4 3.3 copy.31
  54.8 2.4 broadcast_in_dim.5.clone.1
  57.2 6.0 %scatter_fusion = bf16[32,256,256]{2,1,0:T(8,128)(2,1)} fusion(bf16[32,256,256]{2,1,0:T(8,128)(2,1)} %broadcast_in_dim.5.clone.1, s32[16]{0:T(128)S(1)} %fusion.35, bf16[16,256,256]{2,1,0:T(8,128)(2,1)} %bitcast.62), kind=kCustom, calls=%fused_computation.2 | custom fusion | bytes 6291520 | tf_op jit(solution)/shard_map/scatter | solution.py:107
  63.1 73.3 %all-to-all-done.2 = bf16[32,1,256,256]{3,2,1,0:T(8,128)(2,1)} async-done(((bf16[32,1,256,256]{3,2,1,0:T(8,128)(2,1)}), bf16[32,1,256,256]{3,2,1,0:T(8,128)(2,1)}, u32[]{:S(2)}, u32[]{:S(2)}) %all-to-all-start.2) | async-done | bytes 4194336 | tf_op jit(solution)/shard_map/all_to_all | solution.py:116
  136.5 12.8 %all-to-all-start.1 = ((bf16[32,1,256,256]{3,2,1,0:T(8,128)(2,1)}), bf16[32,1,256,256]{3,2,1,0:T(8,128)(2,1)}, u32[]{:S(2)}, u32[]{:S(2)}) async-start(bf16[32,1,256,256]{3,2,1,0:T(8,128)(2,1)} %bitcast.58), calls=%async_computation.1 | async-start | bytes 8388608 | tf_op jit(solution)/shard_map/all_to_all | solution.py:115
  149.2 0.3 convert_reduce_fusion
  149.6 89.4 %all-to-all-done.1 = bf16[32,1,256,256]{3,2,1,0:T(8,128)(2,1)} async-done(((bf16[32,1,256,256]{3,2,1,0:T(8,128)(2,1)}), bf16[32,1,256,256]{3,2,1,0:T(8,128)(2,1)}, u32[]{:S(2)}, u32[]{:S(2)}) %all-to-all-start.1) | async-done | bytes 4194336 | tf_op jit(solution)/shard_map/all_to_all | solution.py:115
  238.9 11.6 %fusion = (f32[32,256,256]{2,1,0:T(8,128)}, f32[32,256,256]{2,1,0:T(8,128)}) fusion(bf16[32,1,256,256]{3,2,1,0:T(8,128)(2,1)} %all-to-all-done.2, bf16[32,1,256,256]{3,2,1,0:T(8,128)(2,1)} %all-to-all-done.1), kind=kLoop, calls=%fused_computation.6 | loop fusion | flops 8388608 | bytes 25165824 | tf_op jit(solution)/shard_map/mul | solution.py:127
  250.5 11.0 %fusion.4 = f32[7,256,256]{2,0,1:T(8,128)S(1)} fusion(f32[32,256,256]{2,1,0:T(8,128)} %get-tuple-element.10, f32[32]{0:T(128)S(1)} %convert_reduce_fusion), kind=kOutput, calls=%fused_computation.10 | convolution fusion | flops 176160992 | bytes 10223744 | tf_op jit(solution)/shard_map/st,sxy->txy/dot_general | solution.py:126
  261.6 7.6 %fusion.2 = f32[7,256,256]{2,0,1:T(8,128)S(1)} fusion(f32[32,256,256]{2,1,0:T(8,128)S(1)} %copy-done.2, f32[32]{0:T(128)S(1)} %convert_reduce_fusion), kind=kOutput, calls=%fused_computation.8 | convolution fusion | flops 176160992 | bytes 10223744 | tf_op jit(solution)/shard_map/st,sxy->txy/dot_general | solution.py:129
  269.2 0.5 slice_bitcast_fusion
  269.7 0.5 pad_maximum_fusion
  270.2 0.3 copy.37
  270.5 7.9 %collective-permute-start = (f32[2,3,256,256]{3,2,1,0:T(8,128)S(1)}, f32[2,3,256,256]{3,2,1,0:T(8,128)S(1)}, u32[]{:S(2)}, u32[]{:S(2)}) collective-permute-start(f32[2,3,256,256]{3,2,1,0:T(8,128)S(1)} %copy.37), channel_id=1, source_target_pairs={{0,32},{32,64},{64,96},{96,128},{128,160},{160,192},{192,224},{224... | collective-permute-start | bytes 4718600 | tf_op jit(solution)/shard_map/ppermute | solution.py:18
  278.4 17.3 %collective-permute-done = f32[2,3,256,256]{3,2,1,0:T(8,128)S(1)} collective-permute-done((f32[2,3,256,256]{3,2,1,0:T(8,128)S(1)}, f32[2,3,256,256]{3,2,1,0:T(8,128)S(1)}, u32[]{:S(2)}, u32[]{:S(2)}) %collective-permute-start) | collective-permute-done | bytes 1572896 | tf_op jit(solution)/shard_map/ppermute | solution.py:18
  295.7 0.1 fusion.41
  295.8 0.5 copy.60
  296.4 0.5 copy.61
  296.9 0.7 fusion.14
  297.6 4.3 collective-permute-start.1
  301.9 6.9 %collective-permute-done.1 = bf16[3,256,256]{2,0,1:T(4,128)(2,1)S(1)} collective-permute-done((bf16[3,256,256]{2,0,1:T(4,128)(2,1)S(1)}, bf16[3,256,256]{2,0,1:T(4,128)(2,1)S(1)}, u32[]{:S(2)}, u32[]{:S(2)}) %collective-permute-start.1) | collective-permute-done | bytes 393248 | tf_op jit(solution)/shard_map/ppermute | solution.py:18
  308.8 1.3 convert_bitcast_fusion
  310.1 4.4 %copy.40 = bf16[32,1,256,256]{3,2,1,0:T(8,128)(2,1)} copy(bf16[32,1,256,256]{3,0,2,1:T(8,128)(2,1)S(1)} %convert_bitcast_fusion) | data formatting | bytes 8388608 | tf_op jit(solution)/shard_map/reshape | solution.py:144
  314.6 7.5 %all-to-all-start.3 = ((bf16[32,1,256,256]{3,2,1,0:T(8,128)(2,1)}), bf16[32,1,256,256]{3,2,1,0:T(8,128)(2,1)}, u32[]{:S(2)}, u32[]{:S(2)}) async-start(bf16[32,1,256,256]{3,2,1,0:T(8,128)(2,1)} %copy.40), calls=%async_computation.3 | async-start | bytes 8388608 | tf_op jit(solution)/shard_map/all_to_all | solution.py:143
  322.1 0.9 copy.42
  322.9 98.7 %all-to-all-done.3 = bf16[32,1,256,256]{3,2,1,0:T(8,128)(2,1)} async-done(((bf16[32,1,256,256]{3,2,1,0:T(8,128)(2,1)}), bf16[32,1,256,256]{3,2,1,0:T(8,128)(2,1)}, u32[]{:S(2)}, u32[]{:S(2)}) %all-to-all-start.3) | async-done | bytes 4194336 | tf_op jit(solution)/shard_map/all_to_all | solution.py:143
  421.6 4.2 gather_fusion
  425.8 2.2 convert.2
  428.0 0.0 copy-done.3
  428.0 4.1 fusion.8
  432.2 4.4 %broadcast_in_dim_reshape.3 = bf16[1,1024,1024]{2,1,0:T(8,128)(2,1)} reshape(bf16[4,256,4,256]{3,2,1,0:T(4,128)(2,1)} %fusion.8) | data formatting | bytes 4194304 | tf_op jit(solution)/shard_map/broadcast_in_dim;reshape | solution.py:154
  (9 shorter events, 0.0 us)
Async XLA Ops:
  0.6 17.6 %copy-start = (bf16[1,36]{1,0:T(2,128)(2,1)S(1)}, bf16[1,36]{1,0:T(2,128)(2,1)}, u32[]{:S(2)}) copy-start(bf16[1,36]{1,0:T(2,128)(2,1)} %param.5) | copy-start | bytes 220
  5.3 32.4 %all-to-all-start = ((bf16[32,1,1]{2,1,0:T(2,128)(2,1)}), bf16[32,1,1]{2,1,0:T(2,128)(2,1)S(1)}, u32[]{:S(2)}, u32[]{:S(2)}) async-start(bf16[32,1,1]{2,1,0:T(2,128)(2,1)} %copy.30), calls=%async_computation | async-start | bytes 32768 | tf_op jit(solution)/shard_map/all_to_all | solution.py:117
  37.7 98.8 %all-to-all-start.2 = ((bf16[32,1,256,256]{3,2,1,0:T(8,128)(2,1)}), bf16[32,1,256,256]{3,2,1,0:T(8,128)(2,1)}, u32[]{:S(2)}, u32[]{:S(2)}) async-start(bf16[32,1,256,256]{3,2,1,0:T(8,128)(2,1)} %bitcast.59), calls=%async_computation.2 | async-start | bytes 8388608 | tf_op jit(solution)/shard_map/all_to_all | solution.py:116
  136.5 102.5 %all-to-all-start.1 = ((bf16[32,1,256,256]{3,2,1,0:T(8,128)(2,1)}), bf16[32,1,256,256]{3,2,1,0:T(8,128)(2,1)}, u32[]{:S(2)}, u32[]{:S(2)}) async-start(bf16[32,1,256,256]{3,2,1,0:T(8,128)(2,1)} %bitcast.58), calls=%async_computation.1 | async-start | bytes 8388608 | tf_op jit(solution)/shard_map/all_to_all | solution.py:115
  250.5 11.0 %copy-start.2 = (f32[32,256,256]{2,1,0:T(8,128)S(1)}, f32[32,256,256]{2,1,0:T(8,128)}, u32[]{:S(2)}) copy-start(f32[32,256,256]{2,1,0:T(8,128)} %get-tuple-element.11) | copy-start | bytes 25165828
  270.5 25.2 %collective-permute-start = (f32[2,3,256,256]{3,2,1,0:T(8,128)S(1)}, f32[2,3,256,256]{3,2,1,0:T(8,128)S(1)}, u32[]{:S(2)}, u32[]{:S(2)}) collective-permute-start(f32[2,3,256,256]{3,2,1,0:T(8,128)S(1)} %copy.37), channel_id=1, source_target_pairs={{0,32},{32,64},{64,96},{96,128},{128,160},{160,192},{192,224},{224... | collective-permute-start | bytes 4718600 | tf_op jit(solution)/shard_map/ppermute | solution.py:18
  297.6 11.2 %collective-permute-start.1 = (bf16[3,256,256]{2,0,1:T(4,128)(2,1)S(1)}, bf16[3,256,256]{2,0,1:T(4,128)(2,1)S(1)}, u32[]{:S(2)}, u32[]{:S(2)}) collective-permute-start(bf16[3,256,256]{2,0,1:T(4,128)(2,1)S(1)} %bitcast.65), channel_id=1, source_target_pairs={{32,0},{64,32},{96,64},{128,96},{160,128},{192,160},{224,192},{256... | collective-permute-start | bytes 1179656 | tf_op jit(solution)/shard_map/ppermute | solution.py:18
  314.6 107.1 %all-to-all-start.3 = ((bf16[32,1,256,256]{3,2,1,0:T(8,128)(2,1)}), bf16[32,1,256,256]{3,2,1,0:T(8,128)(2,1)}, u32[]{:S(2)}, u32[]{:S(2)}) async-start(bf16[32,1,256,256]{3,2,1,0:T(8,128)(2,1)} %copy.40), calls=%async_computation.3 | async-start | bytes 8388608 | tf_op jit(solution)/shard_map/all_to_all | solution.py:143
  425.8 2.2 copy-start.3
  428.0 8.6 %copy-start.1 = (bf16[1,36]{1,0:T(2,128)(2,1)S(1)}, bf16[1,36]{1,0:T(2,128)(2,1)}, u32[]{:S(2)}) copy-start(bf16[1,36]{1,0:T(2,128)(2,1)} %param.5) | copy-start | bytes 220
where the time goes:
time: 437 us
  waiting for transfers between devices  286 us (65%)
  starting transfers between devices  54.6 us (12%)
  local copies, waits for them, and re-layouts  48.2 us (11%)
  matrix products  25.9 us (6%)
  other arithmetic  21.3 us (5%)
    all_to_all x1, waiting for transfers between devices, local(): lax.all_to_all(backward.reshape(col_count, capacity, tile_size, tile_size...  98.7 us
    all_to_all x1, waiting for transfers between devices, local(): lax.all_to_all(send_values, 'col', split_axis=0, concat_axis=0, tiled=True)  89.4 us
    all_to_all x1, waiting for transfers between devices, local(): lax.all_to_all(send_power, 'col', split_axis=0, concat_axis=0, tiled=True)  73.3 us
    ppermute x2, waiting for transfers between devices, shifted(): return lax.ppermute(value, axis, pairs)  24.2 us
    all_to_all x1, starting transfers between devices, local(): lax.all_to_all(send_meta, 'col', split_axis=0, concat_axis=0, tiled=True)  12.9 us
    all_to_all x1, starting transfers between devices, local(): lax.all_to_all(send_values, 'col', split_axis=0, concat_axis=0, tiled=True)  12.8 us
    ppermute x2, starting transfers between devices, shifted(): return lax.ppermute(value, axis, pairs)  12.2 us
    mul x1, other arithmetic, local(): got_values * power_wide  11.6 us
  transfers between devices with their start and end apart: 6, of which 5 were waited for; matrix products, arithmetic and copies ran while one was open for 8% of the time, Pallas kernels for 0%

commit v1 on v0

v1 whole, which is shorter than its diff:
```python
import functools
import math

import jax
import jax.numpy as jnp
import numpy as np
from jax import lax
from jax.experimental import pallas as pl
from jax.experimental.pallas import tpu as pltpu
from jax.sharding import PartitionSpec as P

MESH = pl.DeviceIdType.MESH
FT = 4
NPEER = 32
RES = 16
ROWS7 = 7
NT = 2 * ROWS7
GR = 16
SHARED = 3 * 2 * GR
FLOOR = 0.1
HIGHEST = lax.Precision.HIGHEST
F32 = jnp.float32
BF16 = jnp.bfloat16


def zernike_table():
    table = np.zeros((36, 8, 8))
    term = 0
    for degree in range(8):
        for azimuth in range(-degree, degree + 1, 2):
            order = abs(azimuth)
            angular = np.zeros((8, 8))
            for power in range(order + 1):
                weight = math.comb(order, power)
                if azimuth >= 0 and power % 2 == 0:
                    angular[order - power, power] += weight * (-1) ** (power // 2)
                if azimuth < 0 and power % 2 == 1:
                    angular[order - power, power] += weight * (-1) ** ((power - 1) // 2)
            for step in range((degree - order) // 2 + 1):
                radial = (
                    (-1) ** step
                    * math.factorial(degree - step)
                    / (
                        math.factorial(step)
                        * math.factorial((degree + order) // 2 - step)
                        * math.factorial((degree - order) // 2 - step)
                    )
                )
                square = (degree - 2 * step - order) // 2
                for part in range(square + 1):
                    su, sv = 2 * part, 2 * (square - part)
                    table[term, su:, sv:] += (
                        radial * math.comb(square, part) * angular[: 8 - su, : 8 - sv]
                    )
            term += 1
    return table


def to_local_table(tile):
    foot = FT * tile
    table = zernike_table()
    unit = math.sqrt(2.0) / foot
    sigma = unit * tile / 2
    shift = np.zeros((FT, 8, 8))
    for a in range(FT):
        centre = (a * tile + tile / 2 - foot / 2) * unit
        for i in range(8):
            for m in range(i + 1):
                shift[a, i, m] = math.comb(i, m) * centre ** (i - m) * sigma**m
    local = np.einsum("kij,bim,ajn->kabnm", table, shift, shift)
    to_local = np.zeros((36, RES, 128))
    to_local[:, :, :64] = local.reshape(36, RES, 64)
    return to_local.reshape(36, RES * 128).astype(np.float32)


def iota(shape, dim):
    return lax.broadcasted_iota(jnp.int32, shape, dim)


def to_power(base, exponent):
    square = base * base
    low = jnp.where(lax.rem(exponent, 2) == 1, base, 1.0)
    middle = jnp.where(lax.rem(lax.div(exponent, 2), 2) == 1, square, 1.0)
    return low * middle * jnp.where(lax.div(exponent, 4) == 1, square * square, 1.0)


def kernel(
    strips,
    send,
    meta_send,
    joint_hbm,
    ret_recv,
    recv,
    pbuf,
    ret_send,
    meta_recv,
    bbuf,
    xbuf,
    wbuf,
    k2,
    kt,
    rhs,
    weigh,
    w_lo,
    w_hi,
    numer,
    n_lo,
    n_hi,
    ibuf,
    jbuf,
    fwd_s,
    fwd_r,
    fwd_l,
    meta_s,
    meta_r,
    meta_l,
    w_s,
    w_r,
    n_s,
    n_r,
    j_s,
    j_r,
    j_l,
    ret_s,
    ret_r,
    ret_l,
):
    row = lax.axis_index("row")
    col = lax.axis_index("col")
    n_row = lax.axis_size("row")
    tile = recv.shape[-1]
    half = tile // 2
    rr = half // strips
    gg = rr // GR
    groups = half // GR
    nx, nz = NPEER // 8, 8
    px, pz = lax.div(col, nz), lax.rem(col, nz)
    side = lax.div(col, RES)
    up = lax.rem(row + 1, n_row)
    below = lax.rem(row + n_row - 1, n_row)
    partner = lax.rem(col + RES, NPEER)

    def peer(i):
        j = lax.div(i, nx)
        last = lax.div(j, nz - 1)
        near = lax.div(j, 2) + 1
        dz = (near + lax.rem(j, 2) * (nz - 2 * near)) * (1 - last)
        e = lax.rem(i + last, nx)
        dx = e + lax.div(e, 2) * (1 - 2 * lax.rem(e, 2))
        return lax.rem(px + dx, nx) * nz + lax.rem(pz + dz, nz)

    barrier = pltpu.get_barrier_semaphore()

    def greet(i, carry):
        pl.semaphore_signal(barrier, inc=1, device_id=(row, peer(i)), device_id_type=MESH)
        return carry

    lax.fori_loop(0, NPEER - 1, greet, 0)
    pl.semaphore_signal(barrier, inc=1, device_id=(up, col), device_id_type=MESH)
    pl.semaphore_signal(barrier, inc=1, device_id=(below, col), device_id_type=MESH)

    def own_tile(s):
        return pltpu.make_async_copy(send.at[col, s], recv.at[s, col], fwd_l.at[s])

    def own_meta():
        return pltpu.make_async_copy(meta_send.at[lax.rem(col, RES)], meta_recv.at[col], meta_l)

    def own_residual(s):
        return pltpu.make_async_copy(ret_send.at[s, col], ret_recv.at[col, s], ret_l.at[s])

    def forward(s):
        def one(i, carry):
            to = peer(i)
            pltpu.make_async_remote_copy(
                src_ref=send.at[to, s],
                dst_ref=recv.at[s, col],
                send_sem=fwd_s.at[s],
                recv_sem=fwd_r.at[s],
                device_id=(row, to),
                device_id_type=MESH,
            ).start()
            return carry

        lax.fori_loop(0, NPEER - 1, one, 0)
        own_tile(s).start()

    def send_meta(i, carry):
        to = peer(i)
        pltpu.make_async_remote_copy(
            src_ref=meta_send.at[lax.rem(to, RES)],
            dst_ref=meta_recv.at[col],
            send_sem=meta_s,
            recv_sem=meta_r,
            device_id=(row, to),
            device_id_type=MESH,
        ).start()
        return carry

    pl.semaphore_wait(barrier, NPEER + 1)
    lax.fori_loop(0, NPEER - 1, send_meta, 0)
    own_meta().start()

    def forward_strip(s, carry):
        forward(s)
        return carry

    lax.fori_loop(0, strips, forward_strip, 0)

    shape = (128, tile)
    spot = (iota(shape, 1).astype(F32) + (0.5 - tile / 2)) * (2.0 / tile)
    across = jnp.where(iota(shape, 0) < 64, to_power(spot, lax.rem(iota(shape, 0), 8)), 0.0)
    shape = (half, 48)
    spot = ((iota(shape, 0) + side * half).astype(F32) + (0.5 - tile / 2)) * (2.0 / tile)
    whole = to_power(spot, lax.rem(iota(shape, 1), 8))
    first = whole.astype(BF16).astype(F32)
    second = (whole - first).astype(BF16).astype(F32)
    third = whole - first - second
    part = lax.div(iota(shape, 1), 8)
    down = jnp.where(
        part == 5, third, jnp.where(jnp.logical_or(part == 2, part == 4), second, first)
    ).astype(BF16)
    shape = (256, 128)
    spread = jnp.where(iota(shape, 1) == 64 + lax.div(iota(shape, 0), GR), 1.0, 0.0).astype(BF16)

    arrived = meta_recv.at[pl.ds(0, NPEER - 1)]
    pltpu.make_async_copy(arrived, arrived, meta_r).wait()
    own_meta().wait()
    lane = iota((1, 128), 1)
    own_block = lax.div(iota((8, 128), 1), 8) == iota((8, 128), 0)

    def expand(k, carry):
        values = meta_recv[k]
        bbuf[pl.ds(pl.multiple_of(k * 8, 8), 8), :] = jnp.where(
            own_block, jnp.broadcast_to(values, (8, 128)), 0.0
        )
        hot = jnp.where(lane >= 64, values, 0.0)
        xbuf[pl.ds(pl.multiple_of(k * GR, GR), GR), :] = jnp.broadcast_to(hot, (GR, 128)).astype(
            BF16
        )
        return carry

    lax.fori_loop(0, NPEER, expand, 0)
    wbuf[...] = jnp.dot(bbuf[...], across, precision=HIGHEST, preferred_element_type=F32)
    nt = (((1,), (1,)), ((), ()))
    picked = lax.dot_general(xbuf[...], spread, nt, preferred_element_type=F32)
    shape = (NPEER * GR, 256)
    same = lax.rem(iota(shape, 0), GR) == lax.rem(iota(shape, 1), GR)
    kt[...] = jnp.where(same, picked, 0.0).astype(BF16)
    placed = lax.dot_general(spread, xbuf[...], nt, preferred_element_type=F32)
    shape = (256, NPEER * GR)
    same = lax.rem(iota(shape, 0), GR) == lax.rem(iota(shape, 1), GR)
    placed = jnp.where(same, placed, 0.0).astype(BF16)
    k2[:, : NPEER * GR] = placed
    k2[:, NPEER * GR :] = placed

    def beam(k, carry):
        wide = wbuf[pl.ds(pl.multiple_of(k * 8, 8), 8), :]
        one = wide.astype(BF16).astype(F32)
        rest = wide - one
        two = rest.astype(BF16).astype(F32)
        three = rest - two
        terms = jnp.concatenate([one, two, one, three, two, one], axis=0).astype(BF16)
        field = jnp.dot(down, terms, preferred_element_type=F32)
        power = (field * field).astype(BF16)
        pbuf[:, k] = power.reshape(groups, GR, tile)
        return carry

    lax.fori_loop(0, NPEER, beam, 0)

    def add_up(product):
        step = 8
        for c in range(NPEER // step):
            values = product(c * step, (c + 1) * step).reshape(step * GR, tile)
            high = values.astype(BF16)
            low = (values - high.astype(F32)).astype(BF16)
            rhs[c * step * GR : (c + 1) * step * GR, :] = high
            rhs[(NPEER + c * step) * GR : (NPEER + (c + 1) * step) * GR, :] = low
        return jnp.dot(k2[: NT * GR, :], rhs[...], preferred_element_type=F32)

    def weights(g, carry):
        def product(a, b):
            power = pbuf[g, a:b].astype(F32)
            return power * power

        weigh[g] = add_up(product)
        return carry

    lax.fori_loop(0, groups, weights, 0)

    def swap(sums, low, high, send_sems, recv_sems):
        return (
            pltpu.make_async_remote_copy(
                src_ref=sums.at[:, pl.ds(NT * GR - SHARED, SHARED), :],
                dst_ref=low,
                send_sem=send_sems.at[0],
                recv_sem=recv_sems.at[0],
                device_id=(up, col),
                device_id_type=MESH,
            ),
            pltpu.make_async_remote_copy(
                src_ref=sums.at[:, pl.ds(0, SHARED), :],
                dst_ref=high,
                send_sem=send_sems.at[1],
                recv_sem=recv_sems.at[1],
                device_id=(below, col),
                device_id_type=MESH,
            ),
        )

    weigh_swap = swap(weigh, w_lo, w_hi, w_s, w_r)
    for copy in weigh_swap:
        copy.start()

    def sum_strip(s):
        strip = recv.at[s, pl.ds(0, NPEER - 1)]
        pltpu.make_async_copy(strip, strip, fwd_r.at[s]).wait()
        own_tile(s).wait()

        def one(g, carry):
            def product(a, b):
                return recv[s, a:b, g].astype(F32) * pbuf[s * gg + g, a:b].astype(F32)

            numer[s, g] = add_up(product)
            return carry

        lax.fori_loop(0, gg, one, 0)
        for copy in swap(numer.at[s], n_lo.at[s], n_hi.at[s], n_s.at[s], n_r.at[s]):
            copy.start()

    def joint_copies(s):
        rows = pl.ds(pl.multiple_of(side * half + s * rr, GR), rr)
        return (
            pltpu.make_async_copy(jbuf.at[s, side], joint_hbm.at[:, 0, rows, :], j_l.at[s]),
            pltpu.make_async_remote_copy(
                src_ref=jbuf.at[s, 1 - side],
                dst_ref=joint_hbm.at[:, 0, rows, :],
                send_sem=j_s.at[s],
                recv_sem=j_r.at[s],
                device_id=(row, partner),
                device_id_type=MESH,
            ),
        )

    def image_strip(s):
        for copy in swap(numer.at[s], n_lo.at[s], n_hi.at[s], n_s.at[s], n_r.at[s]):
            copy.wait_recv()

        def one(g, carry):
            at = s * gg + g
            last = NT * GR - SHARED
            ibuf[:SHARED, :] = (
                (numer[s, g, :SHARED, :] + n_lo[s, g]) / weigh[at, :SHARED, :]
            ).astype(BF16)
            ibuf[SHARED:last, :] = (numer[s, g, SHARED:last, :] / weigh[at, SHARED:last, :]).astype(
                BF16
            )
            ibuf[last:, :] = ((numer[s, g, last:, :] + n_hi[s, g]) / weigh[at, last:, :]).astype(
                BF16
            )
            for r in range(FT):
                for h in range(2):
                    first = (r * 2 + h) * GR
                    jbuf[s, h, r, pl.ds(pl.multiple_of(g * GR, GR), GR), :] = ibuf[
                        first : first + GR, :
                    ]
            step = 8
            image = ibuf[...]
            for c in range(NPEER // step):
                mine = jnp.dot(
                    kt[c * step * GR : (c + 1) * step * GR, : NT * GR],
                    image,
                    preferred_element_type=F32,
                ).reshape(step, GR, tile)
                some = pl.ds(c * step, step)
                left = recv[s, some, g].astype(F32) - pbuf[at, some].astype(F32) * mine
                ret_send[s, some, g] = left.astype(BF16)
            return carry

        lax.fori_loop(0, gg, one, 0)

        def back(i, carry):
            to = peer(i)
            pltpu.make_async_remote_copy(
                src_ref=ret_send.at[s, to],
                dst_ref=ret_recv.at[col, s],
                send_sem=ret_s.at[s],
                recv_sem=ret_r.at[s],
                device_id=(row, to),
                device_id_type=MESH,
            ).start()
            return carry

        lax.fori_loop(0, NPEER - 1, back, 0)
        own_residual(s).start()
        for copy in joint_copies(s):
            copy.start()

    def finish_weights():
        for copy in weigh_swap:
            copy.wait()
        last = NT * GR - SHARED

        def one(g, carry):
            weigh[g, :SHARED, :] = jnp.maximum(weigh[g, :SHARED, :] + w_lo[g], FLOOR)
            weigh[g, SHARED:last, :] = jnp.maximum(weigh[g, SHARED:last, :], FLOOR)
            weigh[g, last:, :] = jnp.maximum(weigh[g, last:, :] + w_hi[g], FLOOR)
            return carry

        lax.fori_loop(0, groups, one, 0)

    sum_strip(0)
    finish_weights()

    for s in range(1, strips):
        sum_strip(s)
        image_strip(s - 1)
    image_strip(strips - 1)

    sent = meta_recv.at[pl.ds(0, NPEER - 1)]
    pltpu.make_async_copy(sent, sent, meta_s).wait()

    def drain(s, carry):
        sent = recv.at[s, pl.ds(0, NPEER - 1)]
        pltpu.make_async_copy(sent, sent, fwd_s.at[s]).wait()
        sent = ret_send.at[s, pl.ds(0, NPEER - 1)]
        pltpu.make_async_copy(sent, sent, ret_s.at[s]).wait()
        pltpu.make_async_copy(sent, sent, ret_r.at[s]).wait()
        own_residual(s).wait()
        for copy in swap(numer.at[s], n_lo.at[s], n_hi.at[s], n_s.at[s], n_r.at[s]):
            copy.wait_send()
        for copy in joint_copies(s):
            copy.wait()
        return carry

    lax.fori_loop(0, strips, drain, 0)


def gather_kernel(off_ref, coef_ref, to_local_ref, d_hbm, send, meta, held, in_sem, out_sem):
    tile = held.shape[2]
    half = tile // 2
    row = lax.axis_index("row")
    top = off_ref[0, 0]
    start = lax.rem(off_ref[0, 1] + FT * top, NPEER)

    def arrive(q, h):
        t = lax.rem(q - start + NPEER, RES)
        first = pl.multiple_of(lax.div(t, FT) * tile + h * half, GR)
        across = pl.multiple_of(lax.rem(t, FT) * tile, tile)
        to = h * RES + q
        return pltpu.make_async_copy(
            d_hbm.at[0, pl.ds(first, half), pl.ds(across, tile)], held.at[to], in_sem.at[to]
        )

    def leave(to):
        return pltpu.make_async_copy(held.at[to], send.at[to], out_sem.at[to])

    for q in range(RES):
        for h in range(2):
            arrive(q, h).start()
    flat = jnp.dot(
        coef_ref[...].astype(F32), to_local_ref[...], precision=HIGHEST, preferred_element_type=F32
    )
    lane = iota((1, 128), 1)
    for t in range(RES):
        place = lax.rem(start + t, NPEER)
        target = (top - FT * row + t // FT) * 2 + lax.div(place, RES)
        meta[lax.rem(place, RES)] = jnp.where(
            lane == 64 + target, 1.0, flat[:, t * 128 : (t + 1) * 128]
        )
    for q in range(RES):
        for h in range(2):
            arrive(q, h).wait()
            leave(h * RES + q).start()
    for to in range(NPEER):
        leave(to).wait()


def place_kernel(off_ref, joint, back, joint_out, out_hbm, held, image, in_sem, out_sem, image_sem):
    tile = back.shape[2]
    half = tile // 2
    start = lax.rem(off_ref[0, 1] + FT * off_ref[0, 0], NPEER)

    def arrive(t, h):
        q = lax.rem(start + t, RES)
        rows = pl.ds((t // FT) * tile + h * half, half)
        across = pl.ds((t % FT) * tile, tile)
        return pltpu.make_async_copy(
            back.at[h * RES + q], held.at[rows, across], in_sem.at[t * 2 + h]
        )

    def leave(a, h):
        rows = pl.ds(a * tile + h * half, half)
        return pltpu.make_async_copy(held.at[rows, :], out_hbm.at[0, rows, :], out_sem.at[a * 2 + h])

    image_in = pltpu.make_async_copy(joint, image, image_sem.at[0])
    image_out = pltpu.make_async_copy(image, joint_out, image_sem.at[1])
    image_in.start()
    order = [(a, h) for a in range(FT) for h in range(2)]
    for a, h in order:
        for b in range(FT):
            arrive(a * FT + b, h).start()
    image_in.wait()
    image_out.start()
    for a, h in order:
        for b in range(FT):
            arrive(a * FT + b, h).wait()
        leave(a, h).start()
    for a, h in order:
        leave(a, h).wait()
    image_out.wait()


def local(strips, dirty, coefs, offsets):
    foot = dirty.shape[1]
    tile = foot // FT
    half = tile // 2
    rr = half // strips
    gg = rr // GR
    groups = half // GR
    vmem = pltpu.VMEM
    dma = pltpu.SemaphoreType.DMA
    tiles = (strips, NPEER, gg, GR, tile)
    by_peer = (NPEER, strips, gg, GR, tile)
    anywhere = pl.BlockSpec(memory_space=pl.ANY)
    whole = pl.BlockSpec(memory_space=pltpu.VMEM)
    scalars = pl.BlockSpec(memory_space=pltpu.SMEM)
    send, meta = pl.pallas_call(
        gather_kernel,
        out_shape=(
            jax.ShapeDtypeStruct((NPEER, half, tile), BF16),
            jax.ShapeDtypeStruct((RES, 1, 128), F32),
        ),
        in_specs=[scalars, whole, whole, anywhere],
        out_specs=(anywhere, whole),
        scratch_shapes=[vmem((NPEER, half, tile), BF16), dma((NPEER,)), dma((NPEER,))],
        compiler_params=pltpu.CompilerParams(vmem_limit_bytes=60 * 1024 * 1024),
    )(offsets, coefs, jnp.asarray(to_local_table(tile)), dirty)
    joint, back = pl.pallas_call(
        functools.partial(kernel, strips),
        out_shape=(
            jax.ShapeDtypeStruct((FT, 1, tile, tile), BF16),
            jax.ShapeDtypeStruct(by_peer, BF16),
        ),
        in_specs=[anywhere, anywhere],
        out_specs=(anywhere, anywhere),
        scratch_shapes=[
            vmem(tiles, BF16),
            vmem((groups, NPEER, GR, tile), BF16),
            vmem(tiles, BF16),
            vmem((NPEER, 1, 128), F32),
            vmem((NPEER * 8, 128), F32),
            vmem((NPEER * GR, 128), BF16),
            vmem((NPEER * 8, tile), F32),
            vmem((256, 2 * NPEER * GR), BF16),
            vmem((NPEER * GR, 256), BF16),
            vmem((2 * NPEER * GR, tile), BF16),
            vmem((groups, NT * GR, tile), F32),
            vmem((groups, SHARED, tile), F32),
            vmem((groups, SHARED, tile), F32),
            vmem((strips, gg, NT * GR, tile), F32),
            vmem((strips, gg, SHARED, tile), F32),
            vmem((strips, gg, SHARED, tile), F32),
            vmem((NT * GR, tile), BF16),
            vmem((strips, 2, FT, rr, tile), BF16),
            dma((strips,)),
            dma((strips,)),
            dma((strips,)),
            dma,
            dma,
            dma,
            dma((2,)),
            dma((2,)),
            dma((strips, 2)),
            dma((strips, 2)),
            dma((strips,)),
            dma((strips,)),
            dma((strips,)),
            dma((strips,)),
            dma((strips,)),
            dma((strips,)),
        ],
        compiler_params=pltpu.CompilerParams(
            collective_id=0, has_side_effects=True, vmem_limit_bytes=60 * 1024 * 1024
        ),
    )(send.reshape(by_peer), meta)
    return pl.pallas_call(
        place_kernel,
        out_shape=(
            jax.ShapeDtypeStruct((FT, 1, tile, tile), BF16),
            jax.ShapeDtypeStruct((1, foot, foot), BF16),
        ),
        in_specs=[scalars, anywhere, anywhere],
        out_specs=(anywhere, anywhere),
        scratch_shapes=[
            vmem((foot, foot), BF16),
            vmem((FT, 1, tile, tile), BF16),
            dma((NPEER,)),
            dma((2 * FT,)),
            dma((2,)),
        ],
        compiler_params=pltpu.CompilerParams(vmem_limit_bytes=60 * 1024 * 1024),
    )(offsets, joint, back.reshape(NPEER, half, tile))


def solution(mesh, strips=4):
    in_specs = (P(("row", "col"), None, None), P(("row", "col"), None), P(("row", "col"), None))
    out_specs = (P("row", "col", None, None), P(("row", "col"), None, None))
    return jax.shard_map(
        functools.partial(local, strips),
        mesh=mesh,
        in_specs=in_specs,
        out_specs=out_specs,
        check_vma=False,
    )
```

time: 437 us -> 118 us (0.27)
  the two profiles are of different devices: /device:TPU:47 before, /device:TPU:56 now
where the time goes in v1:
time: 118 us; the launch traced here: 115 us
  Pallas kernels  115 us (97%)
    pallas_call x1, Pallas kernels, local(): pl.pallas_call(functools.partial(kernel, strips), out_shape=(jax.ShapeDty...  106 us
    pallas_call x1, Pallas kernels, local(): pl.pallas_call(gather_kernel, out_shape=(jax.ShapeDtypeStruct((NPEER, hal...  4.61 us
    pallas_call x1, Pallas kernels, local(): pl.pallas_call(place_kernel, out_shape=(jax.ShapeDtypeStruct((FT, 1, tile...  4.3 us

profile of v1, /device:TPU:56, one launch (start us, length us, event | category | flops | bytes accessed | tf_op | source)
XLA Modules:
  0.0 115.4 jit_solution(16712938377727816585)
XLA Ops:
  0.6 4.6 %shard_map.59 = (bf16[32,128,256]{2,1,0:T(8,128)(2,1)}, f32[16,1,128]{2,1,0:T(1,128)}) custom-call(s32[1,2]{1,0:T(1,128)} %off_ref.3, bf16[1,36]{1,0:T(2,128)(2,1)} %coef_ref.1, f32[36,2048]{1,0:T(8,128)} %constant.2.clone.to_local_ref, bf16[1,1024,1024]{2,1,0:T(8,128)(2,1)} %d_hbm.1), custom_call_target="tpu_custom_call" | custom-call | tf_op jit(solution)/shard_map/pallas_call | solution.py:527
  5.2 105.8 %shard_map.60 = (bf16[4,1,256,256]{3,2,1,0:T(8,128)(2,1)}, bf16[32,4,2,16,256]{4,3,2,1,0:T(8,128)(2,1)}) custom-call(bf16[32,4,2,16,256]{4,3,2,1,0:T(8,128)(2,1)} %bitcast.3, f32[16,1,128]{2,1,0:T(1,128)} %get-tuple-element.7.meta_send), custom_call_target="tpu_custom_call" | custom-call | tf_op jit(solution)/shard_map/pallas_call | solution.py:538
  111.1 4.3 %shard_map.61 = (bf16[4,1,256,256]{3,2,1,0:T(8,128)(2,1)}, bf16[1,1024,1024]{2,1,0:T(8,128)(2,1)}) custom-call(s32[1,2]{1,0:T(1,128)} %off_ref.3, bf16[4,1,256,256]{3,2,1,0:T(8,128)(2,1)} %get-tuple-element.8.joint, bf16[32,128,256]{2,1,0:T(8,128)(2,1)} %bitcast.2), custom_call_target="tpu_custom_call" | custom-call | tf_op jit(solution)/shard_map/pallas_call | solution.py:586

commit v2 on v1

v2 whole, which is shorter than its diff:
```python
import math

import jax
import jax.numpy as jnp
import numpy as np
from jax import lax
from jax.experimental import pallas as pl
from jax.experimental.pallas import tpu as pltpu
from jax.sharding import PartitionSpec as P

MESH = pl.DeviceIdType.MESH
FT = 4
NPEER = 32
RES = 16
ROWS7 = 7
NT = 2 * ROWS7
GR = 16
SHARED = 3 * 2 * GR
FLOOR = 0.1
AHEAD = 5
LAG = (0, 2, 4, 6, 8)
HIGHEST = lax.Precision.HIGHEST
F32 = jnp.float32
BF16 = jnp.bfloat16


def zernike_table():
    table = np.zeros((36, 8, 8))
    term = 0
    for degree in range(8):
        for azimuth in range(-degree, degree + 1, 2):
            order = abs(azimuth)
            angular = np.zeros((8, 8))
            for power in range(order + 1):
                weight = math.comb(order, power)
                if azimuth >= 0 and power % 2 == 0:
                    angular[order - power, power] += weight * (-1) ** (power // 2)
                if azimuth < 0 and power % 2 == 1:
                    angular[order - power, power] += weight * (-1) ** ((power - 1) // 2)
            for step in range((degree - order) // 2 + 1):
                radial = (
                    (-1) ** step
                    * math.factorial(degree - step)
                    / (
                        math.factorial(step)
                        * math.factorial((degree + order) // 2 - step)
                        * math.factorial((degree - order) // 2 - step)
                    )
                )
                square = (degree - 2 * step - order) // 2
                for part in range(square + 1):
                    su, sv = 2 * part, 2 * (square - part)
                    table[term, su:, sv:] += (
                        radial * math.comb(square, part) * angular[: 8 - su, : 8 - sv]
                    )
            term += 1
    return table


def to_local_table(tile):
    foot = FT * tile
    table = zernike_table()
    unit = math.sqrt(2.0) / foot
    sigma = unit * tile / 2
    shift = np.zeros((FT, 8, 8))
    for a in range(FT):
        centre = (a * tile + tile / 2 - foot / 2) * unit
        for i in range(8):
            for m in range(i + 1):
                shift[a, i, m] = math.comb(i, m) * centre ** (i - m) * sigma**m
    local = np.einsum("kij,bim,ajn->kabnm", table, shift, shift)
    to_local = np.zeros((36, RES, 128))
    to_local[:, :, :64] = local.reshape(36, RES, 64)
    return to_local.reshape(36, RES * 128).astype(np.float32)


def iota(shape, dim):
    return lax.broadcasted_iota(jnp.int32, shape, dim)


def to_power(base, exponent):
    square = base * base
    low = jnp.where(lax.rem(exponent, 2) == 1, base, 1.0)
    middle = jnp.where(lax.rem(lax.div(exponent, 2), 2) == 1, square, 1.0)
    return low * middle * jnp.where(lax.div(exponent, 4) == 1, square * square, 1.0)


def kernel(
    send,
    meta_send,
    joint_hbm,
    back,
    recv,
    beams,
    beams_all,
    ret_send,
    meta_all,
    meta_role,
    bbuf,
    xbuf,
    wbuf,
    k_all,
    k_role,
    kt,
    high,
    low,
    sums,
    from_below,
    partial,
    partial_in,
    img,
    jbuf,
    fwd_s,
    fwd_r,
    fwd_l,
    meta_s,
    meta_r,
    meta_l,
    up_s,
    up_r,
    part_s,
    part_r,
    img_s,
    img_r,
    down_s,
    down_r,
    j_s,
    j_r,
    j_l,
    ret_s,
    ret_r,
    ret_l,
):
    row = lax.axis_index("row")
    col = lax.axis_index("col")
    n_row = lax.axis_size("row")
    strips = recv.shape[0]
    tile = recv.shape[-1]
    half = tile // 2
    nx, nz = NPEER // 8, 8
    px, pz = lax.div(col, nz), lax.rem(col, nz)
    side = lax.div(col, RES)
    up = lax.rem(row + 1, n_row)
    below = lax.rem(row + n_row - 1, n_row)
    partner = lax.rem(col + RES, NPEER)

    def at(x, dz):
        return x * nz + lax.rem(pz + dz + nz, nz)

    def peer(i):
        j = lax.div(i, nx)
        last = lax.div(j, nz - 1)
        near = lax.div(j, 2) + 1
        dz = (near + lax.rem(j, 2) * (nz - 2 * near)) * (1 - last)
        return at(lax.rem(px + gray(i + last), nx), dz)

    def gray(i):
        e = lax.rem(i, nx)
        return e + lax.div(e, 2) * (1 - 2 * lax.rem(e, 2))

    barrier = pltpu.get_barrier_semaphore()

    def greet(i, carry):
        pl.semaphore_signal(barrier, inc=1, device_id=(row, peer(i)), device_id_type=MESH)
        return carry

    lax.fori_loop(0, NPEER - 1, greet, 0)
    pl.semaphore_signal(barrier, inc=1, device_id=(up, col), device_id_type=MESH)
    pl.semaphore_signal(barrier, inc=1, device_id=(below, col), device_id_type=MESH)

    def remote(src, dst, send_sem, recv_sem, to_row, to_col):
        return pltpu.make_async_remote_copy(
            src_ref=src,
            dst_ref=dst,
            send_sem=send_sem,
            recv_sem=recv_sem,
            device_id=(to_row, to_col),
            device_id_type=MESH,
        )

    def roles(dx):
        odd = lax.rem(dx, 2)
        pair = lax.div(px, 2)
        return (
            (2, 1, 4 + px),
            (-2, -1, 24 + px),
            (3, 2, 8 + px),
            (-3, -2, 28 + px),
            (4, 3 + 2 * odd, 12 + 6 * odd + pair),
            (1, 0, px),
            (-1, 0, 20 + px),
            (0, 0, 14 + px),
        )

    def send_roles(source, target, send_sem, recv_sem, local_sem):
        def one(i, carry):
            dx = gray(i)
            x = lax.rem(px + dx, nx)
            for dz, away, slot in roles(dx):
                to, centre = at(x, away), at(x, dz)
                if isinstance(away, int) and away == 0:

                    @pl.when(dx != 0)
                    def _(centre=centre, slot=slot, to=to):
                        remote(source(centre), target(slot), send_sem, recv_sem, row, to).start()
                else:
                    remote(source(centre), target(slot), send_sem, recv_sem, row, to).start()
            return carry

        lax.fori_loop(0, nx, one, 0)
        for copy in own_copies(source, target, local_sem):
            copy.start()

    def own_copies(source, target, local_sem):
        return [
            pltpu.make_async_copy(source(at(px, dz)), target(slot), local_sem.at[n])
            for n, (dz, slot) in enumerate(((1, px), (0, 14 + px), (-1, 20 + px)))
        ]

    def strip_ends(s):
        return (lambda j: send.at[j, s]), (lambda slot: recv.at[s, slot])

    def forward(s):
        send_roles(*strip_ends(s), fwd_s.at[s], fwd_r.at[s], fwd_l.at[s])

    meta_ends = (lambda j: meta_send.at[lax.rem(j, RES)]), (lambda slot: meta_role.at[slot])

    def own_meta():
        return pltpu.make_async_copy(
            meta_send.at[lax.rem(col, RES)], meta_all.at[col], meta_l.at[3]
        )

    def send_meta(i, carry):
        to = peer(i)
        remote(
            meta_send.at[lax.rem(to, RES)], meta_all.at[col], meta_s.at[1], meta_r.at[1], row, to
        ).start()
        return carry

    pl.semaphore_wait(barrier, NPEER + 1)
    send_roles(*meta_ends, meta_s.at[0], meta_r.at[0], meta_l)
    lax.fori_loop(0, NPEER - 1, send_meta, 0)
    own_meta().start()
    ahead = min(AHEAD, strips)

    def forward_strip(s, carry):
        forward(s)
        return carry

    lax.fori_loop(0, ahead, forward_strip, 0)

    shape = (128, tile)
    spot = (iota(shape, 1).astype(F32) + (0.5 - tile / 2)) * (2.0 / tile)
    across = jnp.where(iota(shape, 0) < 64, to_power(spot, lax.rem(iota(shape, 0), 8)), 0.0)
    shape = (half, 48)
    spot = ((iota(shape, 0) + side * half).astype(F32) + (0.5 - tile / 2)) * (2.0 / tile)
    whole = to_power(spot, lax.rem(iota(shape, 1), 8))
    first = whole.astype(BF16).astype(F32)
    second = (whole - first).astype(BF16).astype(F32)
    third = whole - first - second
    part = lax.div(iota(shape, 1), 8)
    down = jnp.where(
        part == 5, third, jnp.where(jnp.logical_or(part == 2, part == 4), second, first)
    ).astype(BF16)
    shape = (256, 128)
    spread = jnp.where(iota(shape, 1) == 64 + lax.div(iota(shape, 0), GR), 1.0, 0.0).astype(BF16)

    remotes = NPEER - 3
    arrived = meta_role.at[pl.ds(0, remotes)]
    pltpu.make_async_copy(arrived, arrived, meta_r.at[0]).wait()
    for copy in own_copies(*meta_ends, meta_l):
        copy.wait()
    arrived = meta_all.at[pl.ds(0, NPEER - 1)]
    pltpu.make_async_copy(arrived, arrived, meta_r.at[1]).wait()
    own_meta().wait()
    lane = iota((1, 128), 1)
    own_block = lax.div(iota((8, 128), 1), 8) == iota((8, 128), 0)

    def expand(k, carry):
        for n, meta in enumerate((meta_role, meta_all)):
            values = meta[k]
            bbuf[n, pl.ds(pl.multiple_of(k * 8, 8), 8), :] = jnp.where(
                own_block, jnp.broadcast_to(values, (8, 128)), 0.0
            )
            hot = jnp.where(lane >= 64, values, 0.0)
            xbuf[n, pl.ds(pl.multiple_of(k * GR, GR), GR), :] = jnp.broadcast_to(
                hot, (GR, 128)
            ).astype(BF16)
        return carry

    lax.fori_loop(0, NPEER, expand, 0)
    nt = (((1,), (1,)), ((), ()))

    def same(shape):
        return lax.rem(iota(shape, 0), GR) == lax.rem(iota(shape, 1), GR)

    for n in range(2):
        wbuf[n] = jnp.dot(bbuf[n], across, precision=HIGHEST, preferred_element_type=F32)
        placed = lax.dot_general(spread, xbuf[n], nt, preferred_element_type=F32)
        placed = jnp.where(same(placed.shape), placed, 0.0)
        if n == 0:
            slot = lax.div(iota(placed.shape, 1), GR)
            before = jnp.where(slot < 14, placed, 0.0).astype(BF16)
            after = jnp.where(slot >= 18, placed, 0.0).astype(BF16)
            centre = jnp.where(jnp.logical_and(slot >= 14, slot < 18), placed, 0.0).astype(BF16)
            k_role[0] = before[:, :256]
            k_role[1] = centre[:, 128:384]
            k_role[2] = after[:, 256:]
            picked = lax.dot_general(xbuf[n], spread, nt, preferred_element_type=F32)
            kt[...] = jnp.where(same(picked.shape), picked, 0.0).astype(BF16)
        else:
            k_all[...] = placed.astype(BF16)

    def beam(k, carry):
        for n, target in enumerate((beams, beams_all)):
            wide = wbuf[n, pl.ds(pl.multiple_of(k * 8, 8), 8), :]
            one = wide.astype(BF16).astype(F32)
            rest = wide - one
            two = rest.astype(BF16).astype(F32)
            three = rest - two
            terms = jnp.concatenate([one, two, one, three, two, one], axis=0).astype(BF16)
            field = jnp.dot(down, terms, preferred_element_type=F32)
            power = (field * field).astype(BF16)
            target[:, k] = power.reshape(strips, GR, tile)
        return carry

    lax.fori_loop(0, NPEER, beam, 0)

    def split(product):
        step = 8
        for c in range(NPEER // step):
            values = product(c * step, (c + 1) * step).reshape(step * GR, tile)
            some = slice(c * step * GR, (c + 1) * step * GR)
            rounded = values.astype(BF16)
            high[some, :] = rounded
            low[some, :] = (values - rounded.astype(F32)).astype(BF16)

    def add_up(matrix, start, size):
        some = slice(start, start + size)
        return jnp.dot(matrix, high[some, :], preferred_element_type=F32) + jnp.dot(
            matrix, low[some, :], preferred_element_type=F32
        )

    last = NT * GR - SHARED
    own = 2 * FT * GR

    def up_copy(s):
        return remote(
            sums.at[s, :, pl.ds(last, SHARED), :],
            from_below.at[s],
            up_s.at[s],
            up_r.at[s],
            up,
            col,
        )

    def partial_copies(s):
        return [
            remote(
                partial.at[s, n],
                partial_in.at[s, n],
                part_s.at[s, n],
                part_r.at[s, n],
                row,
                at(px, away),
            )
            for n, away in enumerate((1, -1))
        ]

    def image_copies(s):
        return [
            remote(
                img.at[s, 1, pl.ds(0, own), :],
                img.at[s, 2 * n, pl.ds(0, own), :],
                img_s.at[s, n],
                img_r.at[s, n],
                row,
                at(px, away),
            )
            for n, away in enumerate((-1, 1))
        ]

    def down_copy(s):
        return remote(
            img.at[s, :, pl.ds(0, SHARED), :],
            img.at[s, :, pl.ds(last, SHARED), :],
            down_s.at[s],
            down_r.at[s],
            below,
            col,
        )

    def joint_copies(s):
        rows = pl.ds(pl.multiple_of(side * half + s * GR, GR), GR)
        return (
            pltpu.make_async_copy(jbuf.at[s, side], joint_hbm.at[:, 0, rows, :], j_l.at[s]),
            remote(
                jbuf.at[s, 1 - side],
                joint_hbm.at[:, 0, rows, :],
                j_s.at[s],
                j_r.at[s],
                row,
                partner,
            ),
        )

    def sum_strip(s):
        strip = recv.at[s, pl.ds(0, remotes)]
        pltpu.make_async_copy(strip, strip, fwd_r.at[s]).wait()
        for copy in own_copies(*strip_ends(s), fwd_l.at[s]):
            copy.wait()
        split(lambda a, b: recv[s, a:b].astype(F32) * beams[s, a:b].astype(F32))
        for n in range(3):
            sums[s, n] = add_up(k_role[n, : NT * GR, :], n * 128, 256)

        def squares(a, b):
            power = beams_all[s, a:b].astype(F32)
            return power * power

        split(squares)
        sums[s, 3] = add_up(k_all[: NT * GR, :], 0, NPEER * GR)
        up_copy(s).start()

    def partial_strip(s):
        up_copy(s).wait_recv()
        for n in range(2):
            partial[s, n, :SHARED, :] = (
                sums[s, 2 * n, :SHARED, :] + from_below[s, 2 * n]
            ).astype(BF16)
            partial[s, n, SHARED:, :] = sums[s, 2 * n, SHARED:own, :].astype(BF16)
        for copy in partial_copies(s):
            copy.start()

    def image_strip(s):
        for copy in partial_copies(s):
            copy.wait_recv()
        off = partial_in[s, 0].astype(F32) + partial_in[s, 1].astype(F32)
        numer = sums[s, 1, :SHARED, :] + from_below[s, 1] + off[:SHARED]
        weigh = jnp.maximum(sums[s, 3, :SHARED, :] + from_below[s, 3], FLOOR)
        img[s, 1, :SHARED, :] = (numer / weigh).astype(BF16)
        numer = sums[s, 1, SHARED:own, :] + off[SHARED:]
        weigh = jnp.maximum(sums[s, 3, SHARED:own, :], FLOOR)
        img[s, 1, SHARED:own, :] = (numer / weigh).astype(BF16)
        for copy in image_copies(s):
            copy.start()
        for r in range(FT):
            for h in range(2):
                first = (r * 2 + h) * GR
                jbuf[s, h, r] = img[s, 1, first : first + GR, :]
        for copy in joint_copies(s):
            copy.start()

    def pass_strip(s):
        for copy in image_copies(s):
            copy.wait_recv()
        down_copy(s).start()

    def own_back(s):
        return [
            pltpu.make_async_copy(
                ret_send.at[s, slot], back.at[at(px, dz), s], ret_l.at[s, n]
            )
            for n, (dz, slot) in enumerate(((1, px), (0, 14 + px), (-1, 20 + px)))
        ]

    def residual_strip(s):
        down_copy(s).wait_recv()
        for n, a, b in ((0, 0, 7), (0, 7, 14), (1, 14, 18), (2, 18, 25), (2, 25, 32)):
            mine = jnp.dot(
                kt[a * GR : b * GR, : NT * GR], img[s, n], preferred_element_type=F32
            ).reshape(b - a, GR, tile)
            left = recv[s, a:b].astype(F32) - beams[s, a:b].astype(F32) * mine
            ret_send[s, a:b] = left.astype(BF16)

        def one(i, carry):
            dx = gray(i)
            x = lax.rem(px + dx, nx)
            odd = lax.rem(dx, 2)
            ways = (
                (1, -1, 4 + x),
                (-1, 1, 24 + x),
                (1, -2, 8 + x),
                (-1, 2, 28 + x),
                (1 - 2 * odd, 5 - 2 * odd, 12 + 6 * odd + lax.div(x, 2)),
                (1, 0, x),
                (-1, 0, 20 + x),
                (0, 0, 14 + x),
            )
            for dz, away, slot in ways:

                def go(dz=dz, away=away, slot=slot):
                    remote(
                        ret_send.at[s, slot],
                        back.at[at(px, dz), s],
                        ret_s.at[s],
                        ret_r.at[s],
                        row,
                        at(x, away),
                    ).start()

                if isinstance(away, int) and away == 0:
                    pl.when(dx != 0)(go)
                else:
                    go()
            return carry

        lax.fori_loop(0, nx, one, 0)
        for copy in own_back(s):
            copy.start()

    stages = (sum_strip, partial_strip, image_strip, pass_strip, residual_strip)

    def step(i, carry):
        for n in (0, 1, 2, 3, 4):
            pl.when(jnp.logical_and(i >= LAG[n], i < strips + LAG[n]))(lambda n=n: stages[n](i - LAG[n]))
        pl.when(i + ahead < strips)(lambda: forward(i + ahead))
        return carry

    lax.fori_loop(0, strips + LAG[-1], step, 0)

    sent = meta_role.at[pl.ds(0, remotes)]
    pltpu.make_async_copy(sent, sent, meta_s.at[0]).wait()
    sent = meta_all.at[pl.ds(0, NPEER - 1)]
    pltpu.make_async_copy(sent, sent, meta_s.at[1]).wait()

    def drain(s, carry):
        sent = recv.at[s, pl.ds(0, remotes)]
        pltpu.make_async_copy(sent, sent, fwd_s.at[s]).wait()
        up_copy(s).wait_send()
        for copy in partial_copies(s):
            copy.wait_send()
        for copy in image_copies(s):
            copy.wait_send()
        down_copy(s).wait_send()
        for copy in joint_copies(s):
            copy.wait()
        sent = ret_send.at[s, pl.ds(0, remotes)]
        pltpu.make_async_copy(sent, sent, ret_s.at[s]).wait()
        pltpu.make_async_copy(sent, sent, ret_r.at[s]).wait()
        for copy in own_back(s):
            copy.wait()
        return carry

    lax.fori_loop(0, strips, drain, 0)


def gather_kernel(off_ref, coef_ref, to_local_ref, d_hbm, send, meta, held, in_sem, out_sem):
    tile = held.shape[2]
    half = tile // 2
    row = lax.axis_index("row")
    top = off_ref[0, 0]
    start = lax.rem(off_ref[0, 1] + FT * top, NPEER)

    def arrive(q, h):
        t = lax.rem(q - start + NPEER, RES)
        first = pl.multiple_of(lax.div(t, FT) * tile + h * half, GR)
        across = pl.multiple_of(lax.rem(t, FT) * tile, tile)
        to = h * RES + q
        return pltpu.make_async_copy(
            d_hbm.at[0, pl.ds(first, half), pl.ds(across, tile)], held.at[to], in_sem.at[to]
        )

    def leave(to):
        return pltpu.make_async_copy(held.at[to], send.at[to], out_sem.at[to])

    for q in range(RES):
        for h in range(2):
            arrive(q, h).start()
    flat = jnp.dot(
        coef_ref[...].astype(F32), to_local_ref[...], precision=HIGHEST, preferred_element_type=F32
    )
    lane = iota((1, 128), 1)
    for t in range(RES):
        place = lax.rem(start + t, NPEER)
        target = (top - FT * row + t // FT) * 2 + lax.div(place, RES)
        meta[lax.rem(place, RES)] = jnp.where(
            lane == 64 + target, 1.0, flat[:, t * 128 : (t + 1) * 128]
        )
    for q in range(RES):
        for h in range(2):
            arrive(q, h).wait()
            leave(h * RES + q).start()
    for to in range(NPEER):
        leave(to).wait()


def place_kernel(off_ref, joint, back, joint_out, out_hbm, held, image, in_sem, out_sem, image_sem):
    tile = back.shape[2]
    half = tile // 2
    start = lax.rem(off_ref[0, 1] + FT * off_ref[0, 0], NPEER)

    def arrive(t, h):
        q = lax.rem(start + t, RES)
        rows = pl.ds((t // FT) * tile + h * half, half)
        across = pl.ds((t % FT) * tile, tile)
        return pltpu.make_async_copy(
            back.at[h * RES + q], held.at[rows, across], in_sem.at[t * 2 + h]
        )

    def leave(a, h):
        rows = pl.ds(a * tile + h * half, half)
        return pltpu.make_async_copy(held.at[rows, :], out_hbm.at[0, rows, :], out_sem.at[a * 2 + h])

    image_in = pltpu.make_async_copy(joint, image, image_sem.at[0])
    image_out = pltpu.make_async_copy(image, joint_out, image_sem.at[1])
    image_in.start()
    order = [(a, h) for a in range(FT) for h in range(2)]
    for a, h in order:
        for b in range(FT):
            arrive(a * FT + b, h).start()
    image_in.wait()
    image_out.start()
    for a, h in order:
        for b in range(FT):
            arrive(a * FT + b, h).wait()
        leave(a, h).start()
    for a, h in order:
        leave(a, h).wait()
    image_out.wait()


def local(dirty, coefs, offsets):
    foot = dirty.shape[1]
    tile = foot // FT
    half = tile // 2
    strips = half // GR
    vmem = pltpu.VMEM
    dma = pltpu.SemaphoreType.DMA
    tiles = (strips, NPEER, GR, tile)
    by_peer = (NPEER, strips, GR, tile)
    anywhere = pl.BlockSpec(memory_space=pl.ANY)
    whole = pl.BlockSpec(memory_space=pltpu.VMEM)
    scalars = pl.BlockSpec(memory_space=pltpu.SMEM)
    send, meta = pl.pallas_call(
        gather_kernel,
        out_shape=(
            jax.ShapeDtypeStruct((NPEER, half, tile), BF16),
            jax.ShapeDtypeStruct((RES, 1, 128), F32),
        ),
        in_specs=[scalars, whole, whole, anywhere],
        out_specs=(anywhere, whole),
        scratch_shapes=[vmem((NPEER, half, tile), BF16), dma((NPEER,)), dma((NPEER,))],
        compiler_params=pltpu.CompilerParams(vmem_limit_bytes=60 * 1024 * 1024),
    )(offsets, coefs, jnp.asarray(to_local_table(tile)), dirty)
    joint, back = pl.pallas_call(
        kernel,
        out_shape=(
            jax.ShapeDtypeStruct((FT, 1, tile, tile), BF16),
            jax.ShapeDtypeStruct(by_peer, BF16),
        ),
        in_specs=[anywhere, anywhere],
        out_specs=(anywhere, anywhere),
        scratch_shapes=[
            vmem(tiles, BF16),
            vmem(tiles, BF16),
            vmem(tiles, BF16),
            vmem(tiles, BF16),
            vmem((NPEER, 1, 128), F32),
            vmem((NPEER, 1, 128), F32),
            vmem((2, NPEER * 8, 128), F32),
            vmem((2, NPEER * GR, 128), BF16),
            vmem((2, NPEER * 8, tile), F32),
            vmem((256, NPEER * GR), BF16),
            vmem((3, 256, 256), BF16),
            vmem((NPEER * GR, 256), BF16),
            vmem((NPEER * GR, tile), BF16),
            vmem((NPEER * GR, tile), BF16),
            vmem((strips, 4, NT * GR, tile), F32),
            vmem((strips, 4, SHARED, tile), F32),
            vmem((strips, 2, 2 * FT * GR, tile), BF16),
            vmem((strips, 2, 2 * FT * GR, tile), BF16),
            vmem((strips, 3, NT * GR, tile), BF16),
            vmem((strips, 2, FT, GR, tile), BF16),
            dma((strips,)),
            dma((strips,)),
            dma((strips, 3)),
            dma((2,)),
            dma((2,)),
            dma((4,)),
            dma((strips,)),
            dma((strips,)),
            dma((strips, 2)),
            dma((strips, 2)),
            dma((strips, 2)),
            dma((strips, 2)),
            dma((strips,)),
            dma((strips,)),
            dma((strips,)),
            dma((strips,)),
            dma((strips,)),
            dma((strips,)),
            dma((strips,)),
            dma((strips, 3)),
        ],
        compiler_params=pltpu.CompilerParams(
            collective_id=0, has_side_effects=True, vmem_limit_bytes=60 * 1024 * 1024
        ),
    )(send.reshape(by_peer), meta)
    return pl.pallas_call(
        place_kernel,
        out_shape=(
            jax.ShapeDtypeStruct((FT, 1, tile, tile), BF16),
            jax.ShapeDtypeStruct((1, foot, foot), BF16),
        ),
        in_specs=[scalars, anywhere, anywhere],
        out_specs=(anywhere, anywhere),
        scratch_shapes=[
            vmem((foot, foot), BF16),
            vmem((FT, 1, tile, tile), BF16),
            dma((NPEER,)),
            dma((2 * FT,)),
            dma((2,)),
        ],
        compiler_params=pltpu.CompilerParams(vmem_limit_bytes=60 * 1024 * 1024),
    )(offsets, joint, back.reshape(NPEER, half, tile))


def solution(mesh):
    in_specs = (P(("row", "col"), None, None), P(("row", "col"), None), P(("row", "col"), None))
    out_specs = (P("row", "col", None, None), P(("row", "col"), None, None))
    return jax.shard_map(
        local, mesh=mesh, in_specs=in_specs, out_specs=out_specs, check_vma=False
    )
```

time: 118 us -> 104 us (0.88); the launches traced: 115 us -> 104 us
  Pallas kernels: 115 us -> 104 us
    pallas_call x1, Pallas kernels: 106 us -> 94.7 us  [local(): pl.pallas_call(kernel, out_shape=(jax.ShapeDtypeStruct((FT, 1, tile, tile...]
where the time goes in v2:
time: 104 us
  Pallas kernels  104 us (100%)
    pallas_call x1, Pallas kernels, local(): pl.pallas_call(kernel, out_shape=(jax.ShapeDtypeStruct((FT, 1, tile, tile...  94.7 us
    pallas_call x1, Pallas kernels, local(): pl.pallas_call(gather_kernel, out_shape=(jax.ShapeDtypeStruct((NPEER, hal...  4.61 us
    pallas_call x1, Pallas kernels, local(): pl.pallas_call(place_kernel, out_shape=(jax.ShapeDtypeStruct((FT, 1, tile...  4.3 us

profile of v2, /device:TPU:56, one launch (start us, length us, event | category | flops | bytes accessed | tf_op | source)
XLA Modules:
  0.0 104.2 jit_solution(15685447043642803427)
XLA Ops:
  0.6 4.6 %shard_map.59 = (bf16[32,128,256]{2,1,0:T(8,128)(2,1)}, f32[16,1,128]{2,1,0:T(1,128)}) custom-call(s32[1,2]{1,0:T(1,128)} %off_ref.3, bf16[1,36]{1,0:T(2,128)(2,1)} %coef_ref.1, f32[36,2048]{1,0:T(8,128)} %constant.2.clone.to_local_ref, bf16[1,1024,1024]{2,1,0:T(8,128)(2,1)} %d_hbm.1), custom_call_target="tpu_custom_call" | custom-call | tf_op jit(solution)/shard_map/pallas_call | solution.py:634
  5.2 94.7 %shard_map.60 = (bf16[4,1,256,256]{3,2,1,0:T(8,128)(2,1)}, bf16[32,8,16,256]{3,2,1,0:T(8,128)(2,1)}) custom-call(bf16[32,8,16,256]{3,2,1,0:T(8,128)(2,1)} %bitcast.3, f32[16,1,128]{2,1,0:T(1,128)} %get-tuple-element.7.meta_send), custom_call_target="tpu_custom_call" | custom-call | tf_op jit(solution)/shard_map/pallas_call | solution.py:645
  99.9 4.3 %shard_map.61 = (bf16[4,1,256,256]{3,2,1,0:T(8,128)(2,1)}, bf16[1,1024,1024]{2,1,0:T(8,128)(2,1)}) custom-call(s32[1,2]{1,0:T(1,128)} %off_ref.3, bf16[4,1,256,256]{3,2,1,0:T(8,128)(2,1)} %get-tuple-element.8.joint, bf16[32,128,256]{2,1,0:T(8,128)(2,1)} %bitcast.2), custom_call_target="tpu_custom_call" | custom-call | tf_op jit(solution)/shard_map/pallas_call | solution.py:699

commit v3 on v2

--- a/solution.py
+++ b/solution.py
@@ -1,3 +1,4 @@
+import functools
 import math
 
 import jax
@@ -18,6 +19,8 @@
 SHARED = 3 * 2 * GR
 FLOOR = 0.1
 AHEAD = 5
+MAIN_VMEM = 44 * 1024 * 1024
+SMALL_VMEM = 16 * 1024 * 1024
 LAG = (0, 2, 4, 6, 8)
 HIGHEST = lax.Precision.HIGHEST
 F32 = jnp.float32
@@ -544,28 +547,24 @@
     lax.fori_loop(0, strips, drain, 0)
 
 
-def gather_kernel(off_ref, coef_ref, to_local_ref, d_hbm, send, meta, held, in_sem, out_sem):
-    tile = held.shape[2]
-    half = tile // 2
+def gather_kernel(off_ref, coef_ref, to_local_ref, d_hbm, send, meta, sem):
+    strips, tile = send.shape[1], send.shape[3]
     row = lax.axis_index("row")
     top = off_ref[0, 0]
     start = lax.rem(off_ref[0, 1] + FT * top, NPEER)
 
-    def arrive(q, h):
+    def move(q, h):
         t = lax.rem(q - start + NPEER, RES)
-        first = pl.multiple_of(lax.div(t, FT) * tile + h * half, GR)
+        first = (lax.div(t, FT) * 2 + h) * strips
         across = pl.multiple_of(lax.rem(t, FT) * tile, tile)
         to = h * RES + q
         return pltpu.make_async_copy(
-            d_hbm.at[0, pl.ds(first, half), pl.ds(across, tile)], held.at[to], in_sem.at[to]
-        )
-
-    def leave(to):
-        return pltpu.make_async_copy(held.at[to], send.at[to], out_sem.at[to])
-
-    for q in range(RES):
-        for h in range(2):
-            arrive(q, h).start()
+            d_hbm.at[pl.ds(first, strips), :, pl.ds(across, tile)], send.at[to], sem.at[to]
+        )
+
+    moves = [move(q, h) for q in range(RES) for h in range(2)]
+    for copy in moves:
+        copy.start()
     flat = jnp.dot(
         coef_ref[...].astype(F32), to_local_ref[...], precision=HIGHEST, preferred_element_type=F32
     )
@@ -576,47 +575,28 @@
         meta[lax.rem(place, RES)] = jnp.where(
             lane == 64 + target, 1.0, flat[:, t * 128 : (t + 1) * 128]
         )
-    for q in range(RES):
-        for h in range(2):
-            arrive(q, h).wait()
-            leave(h * RES + q).start()
-    for to in range(NPEER):
-        leave(to).wait()
-
-
-def place_kernel(off_ref, joint, back, joint_out, out_hbm, held, image, in_sem, out_sem, image_sem):
-    tile = back.shape[2]
-    half = tile // 2
+    for copy in moves:
+        copy.wait()
+
+
+def place_kernel(off_ref, joint, back, joint_out, out_hbm, sem):
+    strips, tile = back.shape[1], back.shape[3]
     start = lax.rem(off_ref[0, 1] + FT * off_ref[0, 0], NPEER)
 
-    def arrive(t, h):
+    def move(t, h):
         q = lax.rem(start + t, RES)
-        rows = pl.ds((t // FT) * tile + h * half, half)
+        rows = pl.ds(((t // FT) * 2 + h) * strips, strips)
         across = pl.ds((t % FT) * tile, tile)
         return pltpu.make_async_copy(
-            back.at[h * RES + q], held.at[rows, across], in_sem.at[t * 2 + h]
-        )
-
-    def leave(a, h):
-        rows = pl.ds(a * tile + h * half, half)
-        return pltpu.make_async_copy(held.at[rows, :], out_hbm.at[0, rows, :], out_sem.at[a * 2 + h])
-
-    image_in = pltpu.make_async_copy(joint, image, image_sem.at[0])
-    image_out = pltpu.make_async_copy(image, joint_out, image_sem.at[1])
-    image_in.start()
-    order = [(a, h) for a in range(FT) for h in range(2)]
-    for a, h in order:
-        for b in range(FT):
-            arrive(a * FT + b, h).start()
-    image_in.wait()
-    image_out.start()
-    for a, h in order:
-        for b in range(FT):
-            arrive(a * FT + b, h).wait()
-        leave(a, h).start()
-    for a, h in order:
-        leave(a, h).wait()
-    image_out.wait()
+            back.at[h * RES + q], out_hbm.at[rows, :, across], sem.at[t * 2 + h]
+        )
+
+    moves = [move(t, h) for t in range(RES) for h in range(2)]
+    moves.append(pltpu.make_async_copy(joint, joint_out, sem.at[NPEER]))
+    for copy in moves:
+        copy.start()
+    for copy in moves:
+        copy.wait()
 
 
 def local(dirty, coefs, offsets):
@@ -628,26 +608,30 @@
     dma = pltpu.SemaphoreType.DMA
     tiles = (strips, NPEER, GR, tile)
     by_peer = (NPEER, strips, GR, tile)
+    footprint = (foot // GR, GR, foot)
+    image = (FT, 1, tile, tile)
     anywhere = pl.BlockSpec(memory_space=pl.ANY)
     whole = pl.BlockSpec(memory_space=pltpu.VMEM)
     scalars = pl.BlockSpec(memory_space=pltpu.SMEM)
+    in_hbm = functools.partial(pltpu.with_memory_space_constraint, memory_space=pltpu.HBM)
+    in_vmem = functools.partial(pltpu.with_memory_space_constraint, memory_space=pltpu.VMEM)
+    offsets = in_hbm(offsets)
     send, meta = pl.pallas_call(
         gather_kernel,
-        out_shape=(
-            jax.ShapeDtypeStruct((NPEER, half, tile), BF16),
-            jax.ShapeDtypeStruct((RES, 1, 128), F32),
-        ),
+        out_shape=(pltpu.VMEM(by_peer, BF16), pltpu.VMEM((RES, 1, 128), F32)),
         in_specs=[scalars, whole, whole, anywhere],
         out_specs=(anywhere, whole),
-        scratch_shapes=[vmem((NPEER, half, tile), BF16), dma((NPEER,)), dma((NPEER,))],
-        compiler_params=pltpu.CompilerParams(vmem_limit_bytes=60 * 1024 * 1024),
-    )(offsets, coefs, jnp.asarray(to_local_table(tile)), dirty)
+        scratch_shapes=[dma((NPEER,))],
+        compiler_params=pltpu.CompilerParams(vmem_limit_bytes=SMALL_VMEM),
+    )(
+        offsets,
+        in_hbm(coefs),
+        in_hbm(jnp.asarray(to_local_table(tile))),
+        in_hbm(dirty.reshape(footprint)),
+    )
     joint, back = pl.pallas_call(
         kernel,
-        out_shape=(
-            jax.ShapeDtypeStruct((FT, 1, tile, tile), BF16),
-            jax.ShapeDtypeStruct(by_peer, BF16),
-        ),
+        out_shape=(pltpu.VMEM(image, BF16), pltpu.VMEM(by_peer, BF16)),
         in_specs=[anywhere, anywhere],
         out_specs=(anywhere, anywhere),
         scratch_shapes=[
@@ -693,26 +677,18 @@
             dma((strips, 3)),
         ],
         compiler_params=pltpu.CompilerParams(
-            collective_id=0, has_side_effects=True, vmem_limit_bytes=60 * 1024 * 1024
+            collective_id=0, has_side_effects=True, vmem_limit_bytes=MAIN_VMEM
         ),
-    )(send.reshape(by_peer), meta)
-    return pl.pallas_call(
+    )(in_vmem(send), in_vmem(meta))
+    joint, residual = pl.pallas_call(
         place_kernel,
-        out_shape=(
-            jax.ShapeDtypeStruct((FT, 1, tile, tile), BF16),
-            jax.ShapeDtypeStruct((1, foot, foot), BF16),
-        ),
+        out_shape=(pltpu.HBM(image, BF16), pltpu.HBM(footprint, BF16)),
         in_specs=[scalars, anywhere, anywhere],
         out_specs=(anywhere, anywhere),
-        scratch_shapes=[
-            vmem((foot, foot), BF16),
-            vmem((FT, 1, tile, tile), BF16),
-            dma((NPEER,)),
-            dma((2 * FT,)),
-            dma((2,)),
-        ],
-        compiler_params=pltpu.CompilerParams(vmem_limit_bytes=60 * 1024 * 1024),
-    )(offsets, joint, back.reshape(NPEER, half, tile))
+        scratch_shapes=[dma((NPEER + 1,))],
+        compiler_params=pltpu.CompilerParams(vmem_limit_bytes=SMALL_VMEM),
+    )(offsets, in_vmem(joint), in_vmem(back))
+    return joint, residual.reshape(1, foot, foot)
 
 
 def solution(mesh):

time: 104 us -> 101 us (0.971)
  Pallas kernels: 104 us -> 99.9 us
    pallas_call x3, Pallas kernels: 104 us -> 99.9 us  [the longest x1 94.4 us: local(): pl.pallas_call(kernel, out_shape=(pltpu.VMEM(image, BF16), pltpu.VMEM(by_...]
where the time goes in v3:
time: 101 us
  Pallas kernels  99.9 us (99%)
    pallas_call x1, Pallas kernels, local(): pl.pallas_call(kernel, out_shape=(pltpu.VMEM(image, BF16), pltpu.VMEM(by_...  94.4 us
    pallas_call x1, Pallas kernels, local(): pl.pallas_call(gather_kernel, out_shape=(pltpu.VMEM(by_peer, BF16), pltpu...  3.09 us
    pallas_call x1, Pallas kernels, local(): pl.pallas_call(place_kernel, out_shape=(pltpu.HBM(image, BF16), pltpu.HBM...  2.44 us

profile of v3, /device:TPU:56, one launch (start us, length us, event | category | flops | bytes accessed | tf_op | source)
XLA Modules:
  0.0 100.6 jit_solution(11783609166342882684)
XLA Ops:
  0.6 3.1 %shard_map.59 = (bf16[32,8,16,256]{3,2,1,0:T(8,128)(2,1)S(1)}, f32[16,1,128]{2,1,0:T(1,128)S(1)}) custom-call(s32[1,2]{1,0:T(1,128)} %off_ref.3, bf16[1,36]{1,0:T(2,128)(2,1)} %coef_ref.1, f32[36,2048]{1,0:T(8,128)} %constant.2.clone.to_local_ref, bf16[64,16,1024]{2,1,0:T(8,128)(2,1)} %bitcast.2), custom_call_target="tpu_custom_call" | custom-call | tf_op jit(solution)/shard_map/pallas_call | solution.py:619
  3.7 94.4 %shard_map.60 = (bf16[4,1,256,256]{3,2,1,0:T(8,128)(2,1)S(1)}, bf16[32,8,16,256]{3,2,1,0:T(8,128)(2,1)S(1)}) custom-call(bf16[32,8,16,256]{3,2,1,0:T(8,128)(2,1)S(1)} %get-tuple-element.8.send, f32[16,1,128]{2,1,0:T(1,128)S(1)} %get-tuple-element.9.meta_send), custom_call_target="tpu_custom_call" | custom-call | tf_op jit(solution)/shard_map/pallas_call | solution.py:632
  98.1 2.4 %shard_map.61 = (bf16[4,1,256,256]{3,2,1,0:T(8,128)(2,1)}, bf16[64,16,1024]{2,1,0:T(8,128)(2,1)}) custom-call(s32[1,2]{1,0:T(1,128)} %off_ref.3, bf16[4,1,256,256]{3,2,1,0:T(8,128)(2,1)S(1)} %get-tuple-element.10.joint, bf16[32,8,16,256]{3,2,1,0:T(8,128)(2,1)S(1)} %get-tuple-element.11.back), custom_call_target="tpu_custom_call" | custom-call | tf_op jit(solution)/shard_map/pallas_call | solution.py:683

commit v4 on v3

--- a/solution.py
+++ b/solution.py
@@ -21,7 +21,7 @@
 AHEAD = 5
 MAIN_VMEM = 44 * 1024 * 1024
 SMALL_VMEM = 16 * 1024 * 1024
-LAG = (0, 2, 4, 6, 8)
+LAG = (0, 2, 3, 5, 6)
 HIGHEST = lax.Precision.HIGHEST
 F32 = jnp.float32
 BF16 = jnp.bfloat16
@@ -547,7 +547,7 @@
     lax.fori_loop(0, strips, drain, 0)
 
 
-def gather_kernel(off_ref, coef_ref, to_local_ref, d_hbm, send, meta, sem):
+def gather_kernel(off_ref, coef_ref, table, d_hbm, send, meta, to_local, sem, table_sem):
     strips, tile = send.shape[1], send.shape[3]
     row = lax.axis_index("row")
     top = off_ref[0, 0]
@@ -563,10 +563,13 @@
         )
 
     moves = [move(q, h) for q in range(RES) for h in range(2)]
+    load = pltpu.make_async_copy(table, to_local, table_sem)
+    load.start()
     for copy in moves:
         copy.start()
+    load.wait()
     flat = jnp.dot(
-        coef_ref[...].astype(F32), to_local_ref[...], precision=HIGHEST, preferred_element_type=F32
+        coef_ref[...].astype(F32), to_local[...], precision=HIGHEST, preferred_element_type=F32
     )
     lane = iota((1, 128), 1)
     for t in range(RES):
@@ -619,9 +622,9 @@
     send, meta = pl.pallas_call(
         gather_kernel,
         out_shape=(pltpu.VMEM(by_peer, BF16), pltpu.VMEM((RES, 1, 128), F32)),
-        in_specs=[scalars, whole, whole, anywhere],
+        in_specs=[scalars, whole, anywhere, anywhere],
         out_specs=(anywhere, whole),
-        scratch_shapes=[dma((NPEER,))],
+        scratch_shapes=[vmem((36, RES * 128), F32), dma((NPEER,)), dma],
         compiler_params=pltpu.CompilerParams(vmem_limit_bytes=SMALL_VMEM),
     )(
         offsets,

time: 101 us -> 100 us (0.990)
  Pallas kernels: 99.9 us -> 98.3 us
    pallas_call x1, Pallas kernels: 94.4 us -> 92.8 us  [local(): pl.pallas_call(kernel, out_shape=(pltpu.VMEM(image, BF16), pltpu.VMEM(by_...]
where the time goes in v4:
time: 100 us; the launch traced here: 98.9 us
  Pallas kernels  98.3 us (98%)
    pallas_call x1, Pallas kernels, local(): pl.pallas_call(kernel, out_shape=(pltpu.VMEM(image, BF16), pltpu.VMEM(by_...  92.8 us
    pallas_call x1, Pallas kernels, local(): pl.pallas_call(gather_kernel, out_shape=(pltpu.VMEM(by_peer, BF16), pltpu...  3.06 us
    pallas_call x1, Pallas kernels, local(): pl.pallas_call(place_kernel, out_shape=(pltpu.HBM(image, BF16), pltpu.HBM...  2.44 us

profile of v4, /device:TPU:56, one launch (start us, length us, event | category | flops | bytes accessed | tf_op | source)
XLA Modules:
  0.0 98.9 jit_solution(267175776071632026)
XLA Ops:
  0.6 3.1 %shard_map.59 = (bf16[32,8,16,256]{3,2,1,0:T(8,128)(2,1)S(1)}, f32[16,1,128]{2,1,0:T(1,128)S(1)}) custom-call(s32[1,2]{1,0:T(1,128)} %off_ref.3, bf16[1,36]{1,0:T(2,128)(2,1)} %coef_ref.1, f32[36,2048]{1,0:T(8,128)} %constant.2.clone.table, bf16[64,16,1024]{2,1,0:T(8,128)(2,1)} %bitcast.2), custom_call_target="tpu_custom_call" | custom-call | tf_op jit(solution)/shard_map/pallas_call | solution.py:622
  3.7 92.8 %shard_map.60 = (bf16[4,1,256,256]{3,2,1,0:T(8,128)(2,1)S(1)}, bf16[32,8,16,256]{3,2,1,0:T(8,128)(2,1)S(1)}) custom-call(bf16[32,8,16,256]{3,2,1,0:T(8,128)(2,1)S(1)} %get-tuple-element.8.send, f32[16,1,128]{2,1,0:T(1,128)S(1)} %get-tuple-element.9.meta_send), custom_call_target="tpu_custom_call" | custom-call | tf_op jit(solution)/shard_map/pallas_call | solution.py:635
  96.5 2.4 %shard_map.61 = (bf16[4,1,256,256]{3,2,1,0:T(8,128)(2,1)}, bf16[64,16,1024]{2,1,0:T(8,128)(2,1)}) custom-call(s32[1,2]{1,0:T(1,128)} %off_ref.3, bf16[4,1,256,256]{3,2,1,0:T(8,128)(2,1)S(1)} %get-tuple-element.10.joint, bf16[32,8,16,256]{3,2,1,0:T(8,128)(2,1)S(1)} %get-tuple-element.11.back), custom_call_target="tpu_custom_call" | custom-call | tf_op jit(solution)/shard_map/pallas_call | solution.py:686

commit v5 on v4

--- a/solution.py
+++ b/solution.py
@@ -18,7 +18,7 @@
 GR = 16
 SHARED = 3 * 2 * GR
 FLOOR = 0.1
-AHEAD = 5
+AHEAD = 4
 MAIN_VMEM = 44 * 1024 * 1024
 SMALL_VMEM = 16 * 1024 * 1024
 LAG = (0, 2, 3, 5, 6)

time: 100 us -> 102 us (1.020)
    pallas_call x1, Pallas kernels: 92.8 us -> 93.8 us  [local(): pl.pallas_call(kernel, out_shape=(pltpu.VMEM(image, BF16), pltpu.VMEM(by_...]
where the time goes in v5:
time: 102 us; the launch traced here: 100 us
  Pallas kernels  99.3 us (97%)
    pallas_call x1, Pallas kernels, local(): pl.pallas_call(kernel, out_shape=(pltpu.VMEM(image, BF16), pltpu.VMEM(by_...  93.8 us
    pallas_call x1, Pallas kernels, local(): pl.pallas_call(gather_kernel, out_shape=(pltpu.VMEM(by_peer, BF16), pltpu...  3.06 us
    pallas_call x1, Pallas kernels, local(): pl.pallas_call(place_kernel, out_shape=(pltpu.HBM(image, BF16), pltpu.HBM...  2.44 us

profile of v5, /device:TPU:56, one launch (start us, length us, event | category | flops | bytes accessed | tf_op | source)
XLA Modules:
  0.0 100.0 jit_solution(14337801716848372998)
XLA Ops:
  0.6 3.1 %shard_map.59 = (bf16[32,8,16,256]{3,2,1,0:T(8,128)(2,1)S(1)}, f32[16,1,128]{2,1,0:T(1,128)S(1)}) custom-call(s32[1,2]{1,0:T(1,128)} %off_ref.3, bf16[1,36]{1,0:T(2,128)(2,1)} %coef_ref.1, f32[36,2048]{1,0:T(8,128)} %constant.2.clone.table, bf16[64,16,1024]{2,1,0:T(8,128)(2,1)} %bitcast.2), custom_call_target="tpu_custom_call" | custom-call | tf_op jit(solution)/shard_map/pallas_call | solution.py:622
  3.7 93.8 %shard_map.60 = (bf16[4,1,256,256]{3,2,1,0:T(8,128)(2,1)S(1)}, bf16[32,8,16,256]{3,2,1,0:T(8,128)(2,1)S(1)}) custom-call(bf16[32,8,16,256]{3,2,1,0:T(8,128)(2,1)S(1)} %get-tuple-element.8.send, f32[16,1,128]{2,1,0:T(1,128)S(1)} %get-tuple-element.9.meta_send), custom_call_target="tpu_custom_call" | custom-call | tf_op jit(solution)/shard_map/pallas_call | solution.py:635
  97.5 2.4 %shard_map.61 = (bf16[4,1,256,256]{3,2,1,0:T(8,128)(2,1)}, bf16[64,16,1024]{2,1,0:T(8,128)(2,1)}) custom-call(s32[1,2]{1,0:T(1,128)} %off_ref.3, bf16[4,1,256,256]{3,2,1,0:T(8,128)(2,1)S(1)} %get-tuple-element.10.joint, bf16[32,8,16,256]{3,2,1,0:T(8,128)(2,1)S(1)} %get-tuple-element.11.back), custom_call_target="tpu_custom_call" | custom-call | tf_op jit(solution)/shard_map/pallas_call | solution.py:686
